TPU v7x, 256 devices: a whole 4x4x8 slice. The times are simulated.
256 devices in a mesh: blk: 32 (over x, z), term: 8 (over y, core).
Axes of the slice: x: 4, y: 4, z: 8, core: 2. Of those that a mesh axis runs over, the one named last changes fastest.
Arguments:
- wave: float32 [8192, 8192], P('blk'), may hold values from -6 to 6
- left_env: float32 [8, 32, 256, 256], P('term', 'blk'), may hold values from -0.375 to 0.375
- right_env: float32 [8, 32, 256, 256], P('term', 'blk'), may hold values from -0.375 to 0.375
- left_dims: int32 [32], replicated, may hold values from 1 to 256, 4096 in all
- right_dims: int32 [32], replicated, may hold values from 1 to 256, 4096 in all
Outputs:
- applied: float32 [8192, 8192], P('term', 'blk')
Inputs may be any that keep to these rules, and one draw needn't show every extreme that they name: `left_dims`: each sector dimension is at least 1 and at most 256; some sector has exactly 256; the dims of one side sum to 4096. `right_dims`: as for left_dims.
All inputs are finite; a program needn't handle non-finite values.
Results may differ from a plain program's by a relative error of at most 0.0001.
Values sent between devices are 32-bit elements; how exact they have to be, the bound alone decides.
A program may use at most 128 MiB of HBM per device.

v0:
```python
import jax
import jax.numpy as jnp
from jax import lax
from jax.sharding import PartitionSpec as P


def sector_mask(dims, width):
    inside = jnp.arange(width, dtype=jnp.int32)[None, :] < dims[:, None]
    return inside.astype(jnp.float32).reshape(-1)


def shards(wave, left_env, right_env, left_dims, right_dims):
    terms_here, sectors_here, width, _ = left_env.shape
    rows_here, bond = wave.shape
    row_full = sector_mask(left_dims, width)
    col_full = sector_mask(right_dims, width)
    blk_index = lax.axis_index("blk")
    term_index = lax.axis_index("term")
    own_rows = lax.dynamic_slice_in_dim(row_full, blk_index * rows_here, rows_here, 0)
    cols_here = sectors_here * width
    own_cols = lax.dynamic_slice_in_dim(col_full, blk_index * cols_here, cols_here, 0)
    masked = wave * own_rows[:, None] * col_full[None, :]
    out_rows = bond // lax.axis_size("term")
    term_rows = lax.dynamic_slice_in_dim(row_full, term_index * out_rows, out_rows, 0)
    columns = lax.all_to_all(masked, "blk", split_axis=1, concat_axis=0, tiled=True)
    piece = lax.all_gather(left_env, "blk", axis=1, tiled=True)
    count = piece.shape[1]
    rows = columns
    rows = rows.reshape(count, width, cols_here)
    part = jnp.einsum("ksab,sbc->ksac", piece, rows, precision=lax.Precision.HIGHEST)
    left_part = part.reshape(terms_here, count * width, cols_here)
    count = out_rows * lax.axis_size("term")
    rows = left_part
    rows = rows.reshape(terms_here, count, sectors_here, width)
    product = jnp.einsum("krsb,ksab->rsa", rows, right_env, precision=lax.Precision.HIGHEST)
    summed = lax.psum_scatter(
        product.reshape(count, cols_here), "term", scatter_dimension=0, tiled=True
    )
    return summed * term_rows[:, None] * own_cols[None, :]


def solution(mesh):
    placed = (P("blk", None), P("term", "blk", None, None), P("term", "blk", None, None), P(), P())
    return jax.shard_map(
        shards, mesh=mesh, in_specs=placed, out_specs=P("term", "blk"), check_vma=False
    )
```

profile of v0, /device:TPU:35, one launch (start us, length us, event | category | flops | bytes accessed | tf_op | source)
XLA Modules:
  0.0 358.7 jit_solution(8603771521409190914)
XLA Ops:
  6.5 0.0 copy-start
  6.5 0.0 all-gather.2.cloned.1.call-start
  6.5 0.7 all-gather.2.cloned.1.call-update
  7.3 0.7 convert_bitcast_fusion.1
  8.0 0.7 convert_bitcast_fusion
  8.8 9.0 %copy.8 = f32[256,8192]{0,1:T(8,128)} copy(f32[256,8192]{1,0:T(8,128)} %param.5) | data formatting | bytes 16777216 | tf_op args[0]
  17.8 0.1 dynamic_slice.9
  17.8 6.0 %multiply_multiply_fusion = f32[256,8192]{0,1:T(8,128)} fusion(f32[256,8192]{0,1:T(8,128)} %copy.8, f32[8192]{0:T(1024)S(1)} %bitcast.26, f32[256]{0:T(256)S(1)} %dynamic_slice.9), kind=kLoop, calls=%fused_computation.3 | loop fusion | flops 4194304 | bytes 16811008 | tf_op jit(solution)/shard_map/mul | solution.py:22
  23.9 9.1 %copy.9 = f32[256,32,256]{2,0,1:T(8,128)} copy(f32[256,32,256]{0,2,1:T(8,128)} %bitcast.24) | data formatting | bytes 16777216 | tf_op jit(solution)/shard_map/all_to_all | solution.py:25
  32.9 10.7 %all-to-all-start = ((f32[256,32,256]{2,0,1:T(8,128)}), f32[256,32,256]{2,0,1:T(8,128)}, u32[]{:S(2)}, u32[]{:S(2)}) async-start(f32[256,32,256]{2,0,1:T(8,128)} %copy.9), calls=%async_computation | async-start | bytes 16777216 | tf_op jit(solution)/shard_map/all_to_all | solution.py:25
  43.7 0.0 reduce-scatter.2.cloned.1.call-start
  43.7 175.9 %all-gather.2.cloned.1.call-done = f32[1,32,256,256]{3,2,0,1:T(8,128)} async-done(((f32[1,1,256,256]{3,2,0,1:T(8,128)}), f32[1,32,256,256]{3,2,0,1:T(8,128)}) %all-gather.2.cloned.1.call-update) | async-done | bytes 8388624 | tf_op jit(solution)/shard_map/all_gather | solution.py:26
  219.6 48.9 %all-to-all-done = f32[256,32,256]{2,0,1:T(8,128)} async-done(((f32[256,32,256]{2,0,1:T(8,128)}), f32[256,32,256]{2,0,1:T(8,128)}, u32[]{:S(2)}, u32[]{:S(2)}) %all-to-all-start) | async-done | bytes 8388640 | tf_op jit(solution)/shard_map/all_to_all | solution.py:25
  268.5 13.8 %fusion = f32[32,256,256]{1,2,0:T(8,128)S(1)} fusion(f32[1,32,256,256]{3,2,0,1:T(8,128)} %all-gather.2.cloned.1.call-done, f32[256,32,256]{2,0,1:T(8,128)} %all-to-all-done), kind=kOutput, calls=%fused_computation | convolution fusion | flops 6442450944 | bytes 25165824 | tf_op jit(solution)/shard_map/ksab,sbc->ksac/dot_general | solution.py:30
  282.3 0.0 copy-done
  282.3 8.9 %fusion.3 = f32[8192,256]{1,0:T(8,128)} fusion(f32[8192,256]{1,0:T(8,128)S(1)} %bitcast.23, f32[1,1,256,256]{3,2,1,0:T(8,128)S(1)} %copy-done), kind=kOutput, calls=%fused_computation.5 | convolution fusion | flops 6442450944 | bytes 17039360 | tf_op jit(solution)/shard_map/krsb,ksab->rsa/dot_general | solution.py:35
  291.2 0.0 reduce-scatter.2.cloned.1.call-update
  291.3 0.1 dynamic_slice.11
  291.4 58.1 %reduce-scatter.2.cloned.1.call-done = f32[1024,256]{1,0:T(8,128)} async-done(((f32[8192,256]{1,0:T(8,128)}), f32[1024,256]{1,0:T(8,128)}) %reduce-scatter.2.cloned.1.call-update) | async-done | bytes 1048592 | tf_op jit(solution)/shard_map/reduce_scatter | solution.py:36
  349.5 2.4 multiply_multiply_fusion.1
  (3 shorter events, 0.0 us)
Async XLA Ops:
  6.5 275.8 %copy-start = (f32[1,1,256,256]{3,2,1,0:T(8,128)S(1)}, f32[1,1,256,256]{3,2,1,0:T(8,128)}, u32[]{:S(2)}) copy-start(f32[1,1,256,256]{3,2,1,0:T(8,128)} %param.7) | copy-start | bytes 786436
  6.5 213.1 %all-gather.2.cloned.1.call-start = ((), (), s32[]{:S(2)}) async-start(), calls=%async_computation.2 | async-start | bytes 8650752 | tf_op jit(solution)/shard_map/all_gather | solution.py:26
  32.9 235.6 %all-to-all-start = ((f32[256,32,256]{2,0,1:T(8,128)}), f32[256,32,256]{2,0,1:T(8,128)}, u32[]{:S(2)}, u32[]{:S(2)}) async-start(f32[256,32,256]{2,0,1:T(8,128)} %copy.9), calls=%async_computation | async-start | bytes 16777216 | tf_op jit(solution)/shard_map/all_to_all | solution.py:25
  43.7 305.8 %reduce-scatter.2.cloned.1.call-start = ((), (), s32[]{:S(2)}) async-start(), calls=%async_computation.3 | async-start | bytes 9437184 | tf_op jit(solution)/shard_map/reduce_scatter | solution.py:36
Sparse Core Ops, SparseCore 0:
  10.0 209.5 all-gather.1
  291.4 58.0 reduce-scatter.1
where the time goes:
time: 360 us; the launch traced here: 359 us
  waiting for transfers between devices  284 us (79%)
  matrix products  22.7 us (6%)
  local copies, waits for them, and re-layouts  18.2 us (5%)
  between operations  13.4 us (4%)
  starting transfers between devices  10.8 us (3%)
  other arithmetic  9.89 us (3%)
    all_gather x1, waiting for transfers between devices, shards(): piece = lax.all_gather(left_env, 'blk', axis=1, tiled=True)  176 us
    reduce_scatter x1, waiting for transfers between devices, shards(): lax.psum_scatter(product.reshape(count, cols_here), 'term', scatter_dimen...  58.1 us
    all_to_all x1, waiting for transfers between devices, shards(): lax.all_to_all(masked, 'blk', split_axis=1, concat_axis=0, tiled=True)  48.9 us
    dot_general x1, matrix products, shards(): jnp.einsum('ksab,sbc->ksac', piece, rows, precision=lax.Precision.HIGHEST)  13.8 us
    all_to_all x1, starting transfers between devices, shards(): lax.all_to_all(masked, 'blk', split_axis=1, concat_axis=0, tiled=True)  10.7 us
    all_to_all x1, local copies, waits for them, and re-layouts, shards(): lax.all_to_all(masked, 'blk', split_axis=1, concat_axis=0, tiled=True)  9.06 us
    unnamed x5, local copies, waits for them, and re-layouts  9.03 us
    dot_general x1, matrix products, shards(): jnp.einsum('krsb,ksab->rsa', rows, right_env, precision=lax.Precision.HIG...  8.93 us
  transfers between devices with their start and end apart: 3, of which 3 were waited for; matrix products, arithmetic and copies ran while one was open for 7% of the time, Pallas kernels for 0%

commit v1 on v0

v1 whole, which is shorter than its diff:
```python
import jax
import jax.numpy as jnp
from jax import lax
from jax.experimental import pallas as pl
from jax.experimental.pallas import tpu as pltpu
from jax.sharding import PartitionSpec as P

X, Y, Z = 4, 4, 8
SEC = 256
HALF = SEC // 2
RA = 192
RB = SEC - RA
CHUNKS = 16
EARLY = 6
LAG = 6
F32, BF16 = jnp.float32, jnp.bfloat16
MESH = pl.DeviceIdType.MESH


def device(x, y, z, c):
    return {"blk": x * Z + z, "term": y * 2 + c}


def rem(a, n):
    return lax.rem(a, jnp.int32(n))


def div(a, n):
    return lax.div(a, jnp.int32(n))


def split(a):
    high = a.astype(BF16)
    return high, (a - high.astype(F32)).astype(BF16)


def dot3(a, b, dims):
    (ah, al), (bh, bl) = a, b
    out = lax.dot_general(ah, bh, (dims, ((), ())), preferred_element_type=F32)
    out += lax.dot_general(ah, bl, (dims, ((), ())), preferred_element_type=F32)
    return out + lax.dot_general(al, bh, (dims, ((), ())), preferred_element_type=F32)


def received(ref, sem):
    pltpu.make_async_copy(ref, ref, sem).wait()


def kernel(
    ldims, rdims, wave, left, right, out,
    lbuf, rbuf, wbuf, wh, wl, rh, rl, acc,
    l1_s, ring_s, sib_s, l_r, sib_r,
    ra1_s, ra2_s, ra_r, rb1_s, rb1_r, rb2_s, rb2_r,
    w_s, w_r, o_s, o_r,
):
    blk, term = lax.axis_index("blk"), lax.axis_index("term")
    x, z = div(blk, Z), rem(blk, Z)
    y, c = div(term, 2), rem(term, 2)
    zpair, odd = div(z, 2), rem(z, 2)
    xpair, xodd = div(x, 2), rem(x, 2)
    ypair, yodd = div(y, 2), rem(y, 2)
    sibling = device(x, y, z, 1 - c)
    r_owner = c == xpair

    home = rem(z + 2 * rem(y + 2 * odd + c, 4), Z)
    l1_self = (zpair == y) & (home == z)
    l1_to = device(x, zpair, home, c)

    def term_pair(zh, core):
        return rem(div(zh, 2) - y - 2 * rem(zh, 2) - core + 8, 4)

    l1_from = device(x, term_pair(z, c), 2 * y + odd, c)

    def w_to(j):
        return device(x, zpair, rem(z + j, Z), ypair)

    def w_from(i):
        return device(x, 2 * c + i // 4, 2 * y + (i // 2) % 2, i % 2)

    w_self = (zpair == y) & (ypair == c)

    bar = pltpu.get_barrier_semaphore()

    def hello(target):
        pl.semaphore_signal(bar, inc=1, device_id=target, device_id_type=MESH)

    def hello_plane(i, carry):
        hello(device(rem(x + div(i, 8), X), rem(y + rem(div(i, 2), 4), Y), z, rem(c + rem(i, 2), 2)))
        return carry

    lax.fori_loop(1, 32, hello_plane, 0)
    hello(device(x, y, rem(z + 1, Z), c))
    hello(device(x, y, rem(z + Z - 1, Z), c))

    @pl.when(jnp.logical_not(l1_self))
    def _():
        hello(l1_to)
        hello(l1_from)

    for j in range(1, 8):
        hello(w_to(j))
    for i in range(8):
        pl.when(jnp.logical_not((i // 4 == yodd) & ((i // 2) % 2 == odd) & (i % 2 == c) & w_self))(
            lambda i=i: hello(w_from(i))
        )
    pl.when(jnp.logical_not(w_self))(lambda: hello(w_to(0)))
    pl.semaphore_wait(
        bar,
        31 + 2 + 16 + 2 - 2 * l1_self.astype(jnp.int32) - 2 * w_self.astype(jnp.int32),
    )

    def send(src, dst, send_sem, recv_sem, target, own=None):
        copy = pltpu.make_async_remote_copy(
            src_ref=src, dst_ref=dst, send_sem=send_sem, recv_sem=recv_sem,
            device_id=target, device_id_type=MESH,
        )
        if own is None:
            copy.start()
            return copy.wait_send
        pl.when(own)(lambda: pltpu.make_async_copy(src, dst, recv_sem).start())
        pl.when(jnp.logical_not(own))(copy.start)
        return lambda: pl.when(jnp.logical_not(own))(copy.wait_send)

    drains = []
    for h in range(2):
        rows = pl.ds(h * HALF, HALF)
        drains.append(send(
            left.at[0, 0, rows], lbuf.at[home, c, rows], l1_s.at[h], l_r.at[h], l1_to, l1_self))
    for j in range(4):
        own = (r_owner if j == 0 else None)
        drains.append(send(
            right.at[0, 0, pl.ds(0, RA)], rbuf.at[xodd, term, pl.ds(0, RA)],
            ra1_s.at[j], ra_r.at[xodd, term], device(x, rem(y + j, Y), z, xpair), own))
        drains.append(send(
            right.at[0, 0, pl.ds(RA, RB)], rbuf.at[xodd, term, pl.ds(RA, RB)],
            rb1_s.at[j], rb1_r.at[xodd, c], device(rem(x + j, X), y, z, xpair), own))
    for j in (1, 7, 2, 6, 3, 5, 4, 0):
        col = rem(z + j, Z)
        rows = pl.ds(pl.multiple_of(c * HALF, HALF), HALF)
        drains.append(send(
            wave.at[rows, pl.ds(pl.multiple_of((y * Z + col) * SEC, SEC), SEC)],
            wbuf.at[odd, yodd, rows], w_s.at[j], w_r.at[odd, yodd, c], w_to(j),
            w_self if j == 0 else None))

    acc[...] = jnp.zeros_like(acc)

    def ring(zh, rows, later, up):
        target = device(x, y, rem(z + jnp.where(up, 1, Z - 1), Z), c)
        send(lbuf.at[zh, c, rows], lbuf.at[zh, c, rows], ring_s.at[later], l_r.at[later], target)

    def to_sibling(n, zh, rows):
        send(lbuf.at[zh, c, rows], lbuf.at[zh, c, rows], sib_s.at[n], sib_r.at[n], sibling)

    for n, first, second in ((0, 2, 5), (1, 4, 3)):
        rows = pl.ds(n * HALF, HALF)
        received(lbuf.at[z, c, rows], l_r.at[n])
        ring(z, rows, first, True)
        ring(z, rows, second, False)
        to_sibling(n, z, rows)

    for s in range(2):
        for i in range(2):
            received(rbuf.at[s, 2 * y + i, pl.ds(RA, RB)], rb1_r.at[s, i])
    own_k = pl.ds(2 * y, 2)
    for j in range(1, 4):
        part = rbuf.at[:, own_k, pl.ds(RA, RB)]
        drains.append(send(part, part, rb2_s.at[j], rb2_r.at[j], device(x, rem(y + j, Y), z, c)))

    @pl.when(r_owner)
    def _():
        def forward(k, carry):
            part = rbuf.at[xodd, k, pl.ds(0, RA)]
            received(part, ra_r.at[xodd, k])
            for j in range(1, 4):
                send(part, part, ra2_s.at[j, k], ra_r.at[xodd, k], device(rem(x + j, X), y, z, c))
            return carry
        lax.fori_loop(0, 8, forward, 0)

    def place(n):
        m = jnp.maximum(n - 2, 0)
        d, r = div(m, 4) + 1, rem(m, 4)
        first = n < 2
        up = rem(r, 2) == 0
        h = jnp.where(first, n, ((r == 1) | (r == 2)).astype(jnp.int32))
        zh = jnp.where(first, z, rem(z + jnp.where(up, Z - d, d), Z))
        return zh, h, up

    def arrive(n):
        zh, h, up = place(n)
        rows = pl.ds(pl.multiple_of(h * HALF, HALF), HALF)
        received(lbuf.at[zh, c, rows], l_r.at[n])
        pl.when(n + 4 < CHUNKS)(lambda: ring(zh, rows, n + 4, up))
        to_sibling(n, zh, rows)

    def compute(n):
        zh, h, _ = place(n)
        rows = pl.ds(pl.multiple_of(h * HALF, HALF), HALF)
        received(lbuf.at[zh, 1 - c, rows], sib_r.at[n])
        e = rem(zh, 2)
        block = lbuf[zh, :, rows, :].reshape(2 * HALF, SEC)
        mid = dot3(split(block), (wh[e], wl[e]), ((1,), (0,)))
        for s in range(2):
            total = acc[s, e, rows, :]
            for core in range(2):
                k = 2 * term_pair(zh, core) + core
                part = split(mid[core * HALF:(core + 1) * HALF, s * SEC:(s + 1) * SEC])
                total += dot3(part, (rh[s, k], rl[s, k]), ((1,), (1,)))
            acc[s, e, rows, :] = total

    def step(n, carry):
        arrive(n)
        return carry

    lax.fori_loop(2, EARLY, step, 0)

    row_at = lax.broadcasted_iota(jnp.int32, (SEC, SEC), 0)
    col_at = lax.broadcasted_iota(jnp.int32, (SEC, SEC), 1)
    for e in range(2):
        for s in range(2):
            for i in range(2):
                received(wbuf.at[e, s, pl.ds(i * HALF, HALF)], w_r.at[e, s, i])
            inside = (row_at < ldims[x * Z + 2 * y + e]) & (col_at < rdims[(2 * c + s) * Z + z])
            high, low = split(jnp.where(inside, wbuf[e, s], 0.0))
            wh[e, :, s * SEC:(s + 1) * SEC] = high
            wl[e, :, s * SEC:(s + 1) * SEC] = low

    for j in range(1, 4):
        received(rbuf.at[:, pl.ds(2 * rem(y + Y - j, Y), 2), pl.ds(RA, RB)], rb2_r.at[j])
    for s in range(2):
        @pl.when(jnp.logical_not(r_owner & (xodd == s)))
        def _():
            def wait(k, carry):
                received(rbuf.at[s, k, pl.ds(0, RA)], ra_r.at[s, k])
                return carry
            lax.fori_loop(0, 8, wait, 0)

    def split_right(i, carry):
        s, k = div(i, 8), rem(i, 8)
        rh[s, k], rl[s, k] = split(rbuf[s, k])
        return carry

    lax.fori_loop(0, 16, split_right, 0)

    def both(n, carry):
        arrive(n)
        compute(n - LAG)
        return carry

    def late(n, carry):
        compute(n)
        return carry

    lax.fori_loop(EARLY, CHUNKS, both, 0)
    lax.fori_loop(CHUNKS - LAG, CHUNKS, late, 0)

    for i in range(2):
        rows = pl.ds(pl.multiple_of(yodd * 2 * SEC, 2 * SEC), 2 * SEC)
        drains.append(send(
            acc.at[i].reshape(2 * SEC, SEC), out.at[rows], o_s.at[i], o_r.at[yodd],
            device(2 * c + i, x, z, ypair), (x == y) & (c == ypair) & (xodd == i)))
    for drain in drains:
        drain()

    def drain_ring(n, carry):
        part = lbuf.at[0, 0, pl.ds(0, HALF)]
        pl.when(n >= 2)(lambda: pltpu.make_async_copy(part, part, ring_s.at[n]).wait())
        pltpu.make_async_copy(part, part, sib_s.at[n]).wait()
        return carry

    lax.fori_loop(0, CHUNKS, drain_ring, 0)

    @pl.when(r_owner)
    def _():
        def drain_right(k, carry):
            part = rbuf.at[0, 0, pl.ds(0, RA)]
            for j in range(1, 4):
                pltpu.make_async_copy(part, part, ra2_s.at[j, k]).wait()
            return carry
        lax.fori_loop(0, 8, drain_right, 0)

    for j in range(2):
        received(out.at[pl.ds(j * 2 * SEC, 2 * SEC)], o_r.at[j])


def shards(wave, left_env, right_env, left_dims, right_dims):
    dma = pltpu.SemaphoreType.DMA
    vmem, smem, hbm = pltpu.VMEM, pltpu.SMEM, pl.ANY
    raw = pl.pallas_call(
        kernel,
        out_shape=jax.ShapeDtypeStruct((4 * SEC, SEC), F32),
        in_specs=[pl.BlockSpec(memory_space=smem)] * 2 + [pl.BlockSpec(memory_space=hbm)] * 3,
        out_specs=pl.BlockSpec(memory_space=hbm),
        scratch_shapes=[
            vmem((Z, 2, SEC, SEC), F32),
            vmem((2, 8, SEC, SEC), F32),
            vmem((2, 2, SEC, SEC), F32),
            vmem((2, SEC, 2 * SEC), BF16),
            vmem((2, SEC, 2 * SEC), BF16),
            vmem((2, 8, SEC, SEC), BF16),
            vmem((2, 8, SEC, SEC), BF16),
            vmem((2, 2, SEC, SEC), F32),
            dma((2,)), dma((CHUNKS,)), dma((CHUNKS,)), dma((CHUNKS,)), dma((CHUNKS,)),
            dma((4,)), dma((4, 8)), dma((2, 8)), dma((4,)), dma((2, 2)), dma((4,)), dma((4,)),
            dma((8,)), dma((2, 2, 2)), dma((2,)), dma((2,)),
        ],
        compiler_params=pltpu.CompilerParams(
            collective_id=0, has_side_effects=True, vmem_limit_bytes=40 * 2 ** 20),
        cost_estimate=pl.CostEstimate(
            flops=6 * 64 * SEC ** 3, bytes_accessed=4 * 2 ** 20, transcendentals=0),
        name="two_site",
    )(left_dims, right_dims, wave, left_env, right_env)
    blk, term = lax.axis_index("blk"), lax.axis_index("term")
    rows = lax.broadcasted_iota(jnp.int32, (4, SEC, SEC), 1)
    cols = lax.broadcasted_iota(jnp.int32, (4, SEC, SEC), 2)
    own = lax.dynamic_slice_in_dim(left_dims, term * 4, 4, 0)
    inside = (rows < own[:, None, None]) & (cols < right_dims[blk])
    return jnp.where(inside, raw.reshape(4, SEC, SEC), 0.0).reshape(4 * SEC, SEC)


def solution(mesh):
    placed = (P("blk", None), P("term", "blk", None, None), P("term", "blk", None, None), P(), P())
    return jax.shard_map(
        shards, mesh=mesh, in_specs=placed, out_specs=P("term", "blk"), check_vma=False
    )
```

time: 360 us -> 123 us (0.34)
  the two profiles are of different devices: /device:TPU:35 before, /device:TPU:9 now
where the time goes in v1:
time: 123 us; the launch traced here: 122 us
  Pallas kernels  112 us (91%)
  local copies, waits for them, and re-layouts  8.57 us (7%)
  other arithmetic  1.9 us (2%)
    pallas_call x1, Pallas kernels, shards(): pl.pallas_call(kernel, out_shape=jax.ShapeDtypeStruct((4 * SEC, SEC), F32...  112 us
    unnamed x10, local copies, waits for them, and re-layouts  6.59 us

profile of v1, /device:TPU:9, one launch (start us, length us, event | category | flops | bytes accessed | tf_op | source)
XLA Modules:
  0.0 122.5 jit_solution(281985057643536743)
XLA Ops:
  0.0 1.2 %dynamic_slice.7 = s32[1]{0:T(128)} dynamic-slice(s32[32]{0:T(128)} %rdims.1, s32[]{:T(128)S(6)} %select_n.12), dynamic_slice_sizes={1} | dynamic-slice | bytes 12 | tf_op jit(solution)/shard_map/dynamic_slice | solution.py:315
  1.2 0.7 dynamic_slice.6
  2.0 0.6 iota_compare_fusion.1
  2.6 0.1 iota_compare_fusion
  2.7 0.0 copy-start
  2.7 3.4 %copy-done = f32[256,8192]{1,0:T(8,128)S(1)} copy-done((f32[256,8192]{1,0:T(8,128)S(1)}, f32[256,8192]{1,0:T(8,128)}, u32[]{:S(2)}) %copy-start) | copy-done | bytes 8388632
  6.1 0.0 copy-start.1
  6.1 0.9 copy-done.1
  7.0 0.0 copy-start.2
  7.0 0.9 copy-done.2
  8.0 0.0 copy-start.3
  8.0 0.7 copy-done.3
  8.6 0.0 copy-start.4
  8.7 0.7 copy-done.4
  9.3 112.0 %two_site.1 = f32[1024,256]{1,0:T(8,128)S(1)} custom-call(s32[32]{0:T(128)S(1)} %copy-done.3, s32[32]{0:T(128)S(1)} %copy-done.4, f32[256,8192]{1,0:T(8,128)S(1)} %copy-done, f32[1,1,256,256]{3,2,1,0:T(8,128)S(1)} %copy-done.1, f32[1,1,256,256]{3,2,1,0:T(8,128)S(1)} %copy-done.2), custom_call_target="tpu_custom_call" | custom-call | flops 6442450944 | bytes 4194304 | tf_op jit(solution)/shard_map/two_site/pallas_call | solution.py:287
  121.3 1.2 and_select_fusion
  (1 shorter events, 0.0 us)
Async XLA Ops:
  2.7 3.4 %copy-start = (f32[256,8192]{1,0:T(8,128)S(1)}, f32[256,8192]{1,0:T(8,128)}, u32[]{:S(2)}) copy-start(f32[256,8192]{1,0:T(8,128)} %wave.1) | copy-start | bytes 25165828
  6.1 0.9 copy-start.1
  7.0 0.9 copy-start.2
  8.0 0.7 copy-start.3
  8.6 0.7 copy-start.4

commit v2 on v1

v2 whole, which is shorter than its diff:
```python
import jax
import jax.numpy as jnp
from jax import lax
from jax.experimental import pallas as pl
from jax.experimental.pallas import tpu as pltpu
from jax.sharding import PartitionSpec as P

X, Y, Z = 4, 4, 8
SEC = 256
HALF = SEC // 2
RA = 128
RB = SEC - RA
CHUNKS = 16
PIECE = SEC // 4
AT_ONCE = 4
AT_RING = 6
RATE = 3
RELAY = 9
READY = 14
F32, BF16 = jnp.float32, jnp.bfloat16
MESH = pl.DeviceIdType.MESH


def device(x, y, z, c):
    return {"blk": x * Z + z, "term": y * 2 + c}


def rem(a, n):
    return lax.rem(a, jnp.int32(n))


def div(a, n):
    return lax.div(a, jnp.int32(n))


def split(a):
    high = a.astype(BF16)
    return high, (a - high.astype(F32)).astype(BF16)


def dot3(a, b, dims):
    (ah, al), (bh, bl) = a, b
    left = jnp.concatenate([ah, ah, al], dims[0])
    right = jnp.concatenate([bh, bl, bh], dims[1])
    return lax.dot_general(left, right, (((dims[0],), (dims[1],)), ((), ())), preferred_element_type=F32)


def received(ref, sem):
    pltpu.make_async_copy(ref, ref, sem).wait()


def kernel(
    ldims, rdims, wave, left, right, out,
    lbuf, rbuf, wbuf, lh, ll, wh, wl, rh, rl, acc,
    l1_s, ring_s, sib_s, l_r, sib_r,
    ra1_s, ra2_s, ra3_s, ra_r, rb1_s, rb1_r, rb2_s, rb2_r,
    w_s, w_r, o_s, o_r,
):
    blk, term = lax.axis_index("blk"), lax.axis_index("term")
    x, z = div(blk, Z), rem(blk, Z)
    y, c = div(term, 2), rem(term, 2)
    zpair, odd = div(z, 2), rem(z, 2)
    xpair, xodd = div(x, 2), rem(x, 2)
    ypair, yodd = div(y, 2), rem(y, 2)
    sibling = device(x, y, z, 1 - c)
    r_owner = c == xpair

    home = rem(z + 2 * rem(y + 2 * odd + c, 4), Z)
    l1_self = (zpair == y) & (home == z)
    l1_to = device(x, zpair, home, c)

    def term_pair(zh, core):
        return rem(div(zh, 2) - y - 2 * rem(zh, 2) - core + 8, 4)

    l1_from = device(x, term_pair(z, c), 2 * y + odd, c)

    def w_to(j):
        return device(x, zpair, rem(z + j, Z), ypair)

    def w_from(i):
        return device(x, 2 * c + i // 4, 2 * y + (i // 2) % 2, i % 2)

    w_self = (zpair == y) & (ypair == c)

    bar = pltpu.get_barrier_semaphore()

    def hello(target):
        pl.semaphore_signal(bar, inc=1, device_id=target, device_id_type=MESH)

    def hello_plane(i, carry):
        hello(device(rem(x + div(i, 8), X), rem(y + rem(div(i, 2), 4), Y), z, rem(c + rem(i, 2), 2)))
        return carry

    lax.fori_loop(1, 32, hello_plane, 0)
    hello(device(x, y, rem(z + 1, Z), c))
    hello(device(x, y, rem(z + Z - 1, Z), c))

    @pl.when(jnp.logical_not(l1_self))
    def _():
        hello(l1_to)
        hello(l1_from)

    for j in range(1, 8):
        hello(w_to(j))
    for i in range(8):
        pl.when(jnp.logical_not((i // 4 == yodd) & ((i // 2) % 2 == odd) & (i % 2 == c) & w_self))(
            lambda i=i: hello(w_from(i))
        )
    pl.when(jnp.logical_not(w_self))(lambda: hello(w_to(0)))
    pl.semaphore_wait(
        bar,
        31 + 2 + 16 + 2 - 2 * l1_self.astype(jnp.int32) - 2 * w_self.astype(jnp.int32),
    )

    def send(src, dst, send_sem, recv_sem, target, own=None):
        copy = pltpu.make_async_remote_copy(
            src_ref=src, dst_ref=dst, send_sem=send_sem, recv_sem=recv_sem,
            device_id=target, device_id_type=MESH,
        )
        if own is None:
            copy.start()
            return copy.wait_send
        pl.when(own)(lambda: pltpu.make_async_copy(src, dst, recv_sem).start())
        pl.when(jnp.logical_not(own))(copy.start)
        return lambda: pl.when(jnp.logical_not(own))(copy.wait_send)

    drains = []
    for h in range(2):
        rows = pl.ds(h * HALF, HALF)
        drains.append(send(
            left.at[0, 0, rows], lbuf.at[home, c, rows], l1_s.at[h], l_r.at[h], l1_to, l1_self))
    for j in range(4):
        own = (r_owner if j == 0 else None)
        drains.append(send(
            right.at[0, 0, pl.ds(0, RA)], rbuf.at[xodd, term, pl.ds(0, RA)],
            ra1_s.at[j], ra_r.at[xodd, term], device(x, rem(y + j, Y), z, xpair), own))
        drains.append(send(
            right.at[0, 0, pl.ds(RA, RB)], rbuf.at[xodd, term, pl.ds(RA, RB)],
            rb1_s.at[j], rb1_r.at[xodd, c], device(rem(x + j, X), y, z, xpair), own))
    quarter = 2 * yodd + c
    quarter_rows = pl.ds(pl.multiple_of(quarter * PIECE, PIECE), PIECE)

    def spread(i, carry):
        p, i = div(i, 8), rem(i, 8)
        j = jnp.where(i == 7, 0, jnp.where(rem(i, 2) == 0, div(i, 2) + 1, 7 - div(i, 2)))
        col = (2 * ypair + p) * Z + rem(z + j, Z)
        send(
            wave.at[quarter_rows, pl.ds(pl.multiple_of(col * SEC, SEC), SEC)],
            wbuf.at[odd, p, quarter_rows], w_s.at[p, i], w_r.at[p, odd, quarter], w_to(j),
            w_self & (i == 7))
        return carry

    lax.fori_loop(0, AT_ONCE, spread, 0)

    def ring(zh, rows, later, up):
        target = device(x, y, rem(z + jnp.where(up, 1, Z - 1), Z), c)
        send(lbuf.at[zh, c, rows], lbuf.at[zh, c, rows], ring_s.at[later], l_r.at[later], target)

    def to_sibling(n, zh, rows):
        send(lbuf.at[zh, c, rows], lbuf.at[zh, c, rows], sib_s.at[n], sib_r.at[n], sibling)

    for n, first, second in ((0, 2, 5), (1, 4, 3)):
        rows = pl.ds(n * HALF, HALF)
        received(lbuf.at[z, c, rows], l_r.at[n])
        ring(z, rows, first, True)
        ring(z, rows, second, False)
        to_sibling(n, z, rows)

    lax.fori_loop(AT_ONCE, AT_RING, spread, 0)

    for s in range(2):
        for i in range(2):
            received(rbuf.at[s, 2 * y + i, pl.ds(RA, RB)], rb1_r.at[s, i])

    def lower(yk, s):
        return rbuf.at[s, pl.ds(2 * yk, 2), pl.ds(RA, RB)]

    def upper(s, k):
        return rbuf.at[s, k, pl.ds(0, RA)]

    up_y, down_y = rem(y + 1, Y), rem(y + Y - 1, Y)
    up_x, down_x = rem(x + 1, X), rem(x + X - 1, X)
    for s in range(2):
        for way, to in enumerate((up_y, down_y)):
            drains.append(send(lower(y, s), lower(y, s), rb2_s.at[way, s], rb2_r.at[way, s], device(x, to, z, c)))

    @pl.when(r_owner)
    def _():
        def forward(k, carry):
            received(upper(xodd, k), ra_r.at[xodd, k])
            for way, to in enumerate((up_x, down_x)):
                send(upper(xodd, k), upper(xodd, k), ra2_s.at[way, k], ra_r.at[xodd, k], device(to, y, z, c))
            return carry
        lax.fori_loop(0, 8, forward, 0)

    def distance(s):
        return rem(x - (2 * c + s) + X, X)

    def relay():
        received(lower(down_y, 0), rb2_r.at[0, 0])
        drains.append(send(
            lower(down_y, 0), lower(down_y, 0), rb2_s.at[2, 0], rb2_r.at[2, 0], device(x, up_y, z, c)))
        received(lower(up_y, 1), rb2_r.at[1, 1])
        drains.append(send(
            lower(up_y, 1), lower(up_y, 1), rb2_s.at[2, 1], rb2_r.at[2, 1], device(x, down_y, z, c)))
        for s in range(2):
            for d, first, to in ((1, 0, up_x), (3, 1, down_x)):
                @pl.when(distance(s) == d)
                def _():
                    def forward(i, carry):
                        k = 2 * i + first
                        received(upper(s, k), ra_r.at[s, k])
                        send(upper(s, k), upper(s, k), ra3_s.at[s, k], ra_r.at[s, k], device(to, y, z, c))
                        return carry
                    lax.fori_loop(0, 4, forward, 0)

    def place(n):
        m = jnp.maximum(n - 2, 0)
        d, r = div(m, 4) + 1, rem(m, 4)
        first = n < 2
        up = rem(r, 2) == 0
        h = jnp.where(first, n, ((r == 1) | (r == 2)).astype(jnp.int32))
        zh = jnp.where(first, z, rem(z + jnp.where(up, Z - d, d), Z))
        return zh, h, up

    def arrive(n):
        zh, h, up = place(n)
        rows = pl.ds(pl.multiple_of(h * HALF, HALF), HALF)
        received(lbuf.at[zh, c, rows], l_r.at[n])
        pl.when(n + 4 < CHUNKS)(lambda: ring(zh, rows, n + 4, up))
        to_sibling(n, zh, rows)

    def prepare(n):
        zh, h, _ = place(n)
        rows = pl.ds(pl.multiple_of(h * HALF, HALF), HALF)
        received(lbuf.at[zh, 1 - c, rows], sib_r.at[n])
        lh[zh, :, rows, :], ll[zh, :, rows, :] = split(lbuf[zh, :, rows, :])

    def issued(n):
        return jnp.minimum(16, AT_RING + div((n - 1) * RATE, 4))

    def step(n, carry):
        arrive(n)
        lax.fori_loop(issued(n - 1), issued(n), spread, 0)
        prepare(n - 2)
        return carry

    def wait_right():
        received(lower(down_y, 1), rb2_r.at[0, 1])
        received(lower(up_y, 0), rb2_r.at[1, 0])
        for s in range(2):
            received(lower(rem(y + 2, Y), s), rb2_r.at[2, s])

            def wait(k, carry):
                d = distance(s)
                done = (d == 0) | ((d == 1) & (rem(k, 2) == 0)) | ((d == 3) & (rem(k, 2) == 1))
                pl.when(jnp.logical_not(done))(lambda: received(upper(s, k), ra_r.at[s, k]))
                return carry
            lax.fori_loop(0, 8, wait, 0)

    def split_right(i, carry):
        s, k = div(i, 8), rem(i, 8)
        rh[s, k], rl[s, k] = split(rbuf[s, k])
        return carry

    def ready():
        wait_right()
        lax.fori_loop(0, 16, split_right, 0)

    lax.fori_loop(2, RELAY, step, 0)
    relay()
    lax.fori_loop(RELAY, READY, step, 0)
    ready()
    lax.fori_loop(READY, CHUNKS, step, 0)
    lax.fori_loop(issued(CHUNKS - 1), 16, spread, 0)
    prepare(CHUNKS - 2)
    prepare(CHUNKS - 1)

    row_at = lax.broadcasted_iota(jnp.int32, (SEC, SEC), 0)
    col_at = lax.broadcasted_iota(jnp.int32, (SEC, SEC), 1)

    def product(s, e, m):
        zh = 2 * m + e
        flat = (2 * SEC, SEC)
        mid = dot3((lh[zh].reshape(flat), ll[zh].reshape(flat)), (wh[...], wl[...]), (1, 0))
        high, low = split(mid)
        parts = []
        for core in range(2):
            k = 2 * term_pair(zh, core) + core
            rows = slice(core * SEC, (core + 1) * SEC)
            parts.append((high[rows], low[rows], rh[s, k], rl[s, k]))
        (h0, l0, rh0, rl0), (h1, l1, rh1, rl1) = parts
        return dot3(
            (jnp.concatenate([h0, h1], 1), jnp.concatenate([l0, l1], 1)),
            (jnp.concatenate([rh0, rh1], 1), jnp.concatenate([rl0, rl1], 1)), (1, 1))

    for s in range(2):
        for e in range(2):
            inside = (row_at < ldims[x * Z + 2 * y + e]) & (col_at < rdims[(2 * c + s) * Z + z])
            for q in range(4):
                received(wbuf.at[e, s, pl.ds(q * PIECE, PIECE)], w_r.at[s, e, q])
            wh[...], wl[...] = split(jnp.where(inside, wbuf[e, s], 0.0))
            acc[s, e] = product(s, e, 0)
            for m in range(1, 4):
                acc[s, e] += product(s, e, m)
            acc[s, e] = jnp.where(inside, acc[s, e], 0.0)
            send(
                acc.at[s, e], out.at[2 * yodd + e], o_s.at[s, e], o_r.at[2 * yodd + e],
                device(2 * c + s, x, z, ypair), (x == y) & (c == ypair) & (xodd == s))

    for drain in drains:
        drain()
    for s in range(2):
        @pl.when(jnp.logical_not((x == y) & (c == ypair) & (xodd == s)))
        def _():
            for e in range(2):
                received(acc.at[s, e], o_s.at[s, e])

    def drain_wave(i, carry):
        part = wbuf.at[0, 0, pl.ds(0, PIECE)]
        pl.when(jnp.logical_not(w_self & (rem(i, 8) == 7)))(
            lambda: received(part, w_s.at[div(i, 8), rem(i, 8)]))
        return carry

    lax.fori_loop(0, 16, drain_wave, 0)

    def drain_ring(n, carry):
        part = lbuf.at[0, 0, pl.ds(0, HALF)]
        pl.when(n >= 2)(lambda: pltpu.make_async_copy(part, part, ring_s.at[n]).wait())
        pltpu.make_async_copy(part, part, sib_s.at[n]).wait()
        return carry

    lax.fori_loop(0, CHUNKS, drain_ring, 0)

    @pl.when(r_owner)
    def _():
        def drain_right(k, carry):
            for way in range(2):
                received(upper(0, 0), ra2_s.at[way, k])
            return carry
        lax.fori_loop(0, 8, drain_right, 0)

    for s in range(2):
        for d, first in ((1, 0), (3, 1)):
            @pl.when(distance(s) == d)
            def _():
                def drain_relay(i, carry):
                    received(upper(0, 0), ra3_s.at[s, 2 * i + first])
                    return carry
                lax.fori_loop(0, 4, drain_relay, 0)

    for j in range(4):
        received(out.at[j], o_r.at[j])


def shards(wave, left_env, right_env, left_dims, right_dims):
    dma = pltpu.SemaphoreType.DMA
    vmem, smem, hbm = pltpu.VMEM, pltpu.SMEM, pl.ANY
    return pl.pallas_call(
        kernel,
        out_shape=jax.ShapeDtypeStruct((4, SEC, SEC), F32),
        in_specs=[pl.BlockSpec(memory_space=smem)] * 2 + [pl.BlockSpec(memory_space=hbm)] * 3,
        out_specs=pl.BlockSpec(memory_space=vmem),
        scratch_shapes=[
            vmem((Z, 2, SEC, SEC), F32),
            vmem((2, 8, SEC, SEC), F32),
            vmem((2, 2, SEC, SEC), F32),
            vmem((Z, 2, SEC, SEC), BF16),
            vmem((Z, 2, SEC, SEC), BF16),
            vmem((SEC, SEC), BF16),
            vmem((SEC, SEC), BF16),
            vmem((2, 8, SEC, SEC), BF16),
            vmem((2, 8, SEC, SEC), BF16),
            vmem((2, 2, SEC, SEC), F32),
            dma((2,)), dma((CHUNKS,)), dma((CHUNKS,)), dma((CHUNKS,)), dma((CHUNKS,)),
            dma((4,)), dma((2, 8)), dma((2, 8)), dma((2, 8)), dma((4,)), dma((2, 2)), dma((3, 2)), dma((3, 2)),
            dma((2, 8)), dma((2, 2, 4)), dma((2, 2)), dma((4,)),
        ],
        compiler_params=pltpu.CompilerParams(
            collective_id=0, has_side_effects=True, vmem_limit_bytes=60 * 2 ** 20),
        cost_estimate=pl.CostEstimate(
            flops=6 * 64 * SEC ** 3, bytes_accessed=4 * 2 ** 20, transcendentals=0),
        name="two_site",
    )(left_dims, right_dims, wave, left_env, right_env).reshape(4 * SEC, SEC)


def solution(mesh):
    placed = (P("blk", None), P("term", "blk", None, None), P("term", "blk", None, None), P(), P())
    return jax.shard_map(
        shards, mesh=mesh, in_specs=placed, out_specs=P("term", "blk"), check_vma=False
    )
```

time: 123 us -> 86.9 us (0.71)
  the two profiles are of different devices: /device:TPU:9 before, /device:TPU:35 now
where the time goes in v2:
time: 86.9 us; the launch traced here: 86.1 us
  Pallas kernels  83.8 us (96%)
  local copies, waits for them, and re-layouts  2.26 us (3%)
    pallas_call x1, Pallas kernels, shards(): pl.pallas_call(kernel, out_shape=jax.ShapeDtypeStruct((4, SEC, SEC), F32)...  83.8 us
    unnamed x1, local copies, waits for them, and re-layouts  2.26 us

profile of v2, /device:TPU:35, one launch (start us, length us, event | category | flops | bytes accessed | tf_op | source)
XLA Modules:
  0.0 86.1 jit_solution(14019490736388033612)
XLA Ops:
  0.0 83.8 %two_site.1 = f32[4,256,256]{2,1,0:T(8,128)} custom-call(s32[32]{0:T(128)} %ldims.1, s32[32]{0:T(128)} %rdims.1, f32[256,8192]{1,0:T(8,128)} %wave.1, f32[1,1,256,256]{3,2,1,0:T(8,128)} %left.1, f32[1,1,256,256]{3,2,1,0:T(8,128)} %right.1), custom_call_target="tpu_custom_call" | custom-call | flops 6442450944 | bytes 4194304 | tf_op jit(solution)/shard_map/two_site/pallas_call | solution.py:359
  83.8 2.3 %copy.7 = f32[1024,256]{1,0:T(8,128)} copy(f32[1024,256]{1,0:T(8,128)} %bitcast.1) | data formatting | bytes 2097152

commit v3 on v2

--- a/solution.py
+++ b/solution.py
@@ -271,10 +271,10 @@
     relay()
     lax.fori_loop(RELAY, READY, step, 0)
     ready()
-    lax.fori_loop(READY, CHUNKS, step, 0)
-    lax.fori_loop(issued(CHUNKS - 1), 16, spread, 0)
-    prepare(CHUNKS - 2)
-    prepare(CHUNKS - 1)
+    lax.fori_loop(READY, CHUNKS - 2, step, 0)
+    prepare(CHUNKS - 4)
+    prepare(CHUNKS - 3)
+    lax.fori_loop(issued(CHUNKS - 3), issued(CHUNKS - 1), spread, 0)
 
     row_at = lax.broadcasted_iota(jnp.int32, (SEC, SEC), 0)
     col_at = lax.broadcasted_iota(jnp.int32, (SEC, SEC), 1)
@@ -295,7 +295,7 @@
             (jnp.concatenate([rh0, rh1], 1), jnp.concatenate([rl0, rl1], 1)), (1, 1))
 
     for s in range(2):
-        for e in range(2):
+        for e in (1 - odd, odd):
             inside = (row_at < ldims[x * Z + 2 * y + e]) & (col_at < rdims[(2 * c + s) * Z + z])
             for q in range(4):
                 received(wbuf.at[e, s, pl.ds(q * PIECE, PIECE)], w_r.at[s, e, q])
@@ -307,6 +307,12 @@
             send(
                 acc.at[s, e], out.at[2 * yodd + e], o_s.at[s, e], o_r.at[2 * yodd + e],
                 device(2 * c + s, x, z, ypair), (x == y) & (c == ypair) & (xodd == s))
+            if s == 0 and e is not odd:
+                for n in (CHUNKS - 2, CHUNKS - 1):
+                    arrive(n)
+                lax.fori_loop(issued(CHUNKS - 1), 16, spread, 0)
+                for n in (CHUNKS - 2, CHUNKS - 1):
+                    prepare(n)
 
     for drain in drains:
         drain()
@@ -360,7 +366,7 @@
         kernel,
         out_shape=jax.ShapeDtypeStruct((4, SEC, SEC), F32),
         in_specs=[pl.BlockSpec(memory_space=smem)] * 2 + [pl.BlockSpec(memory_space=hbm)] * 3,
-        out_specs=pl.BlockSpec(memory_space=vmem),
+        out_specs=pl.BlockSpec(memory_space=hbm),
         scratch_shapes=[
             vmem((Z, 2, SEC, SEC), F32),
             vmem((2, 8, SEC, SEC), F32),

time: 86.9 us -> 85.8 us (0.987)
  no operation moved by 1% of the time
where the time goes in v3:
time: 85.8 us; the launch traced here: 85.6 us
  Pallas kernels  83.3 us (97%)
  local copies, waits for them, and re-layouts  2.26 us (3%)
    pallas_call x1, Pallas kernels, shards(): pl.pallas_call(kernel, out_shape=jax.ShapeDtypeStruct((4, SEC, SEC), F32)...  83.3 us
    unnamed x1, local copies, waits for them, and re-layouts  2.26 us

profile of v3, /device:TPU:35, one launch (start us, length us, event | category | flops | bytes accessed | tf_op | source)
XLA Modules:
  0.0 85.6 jit_solution(11967119519233282620)
XLA Ops:
  0.0 83.3 %two_site.1 = f32[4,256,256]{2,1,0:T(8,128)} custom-call(s32[32]{0:T(128)} %ldims.1, s32[32]{0:T(128)} %rdims.1, f32[256,8192]{1,0:T(8,128)} %wave.1, f32[1,1,256,256]{3,2,1,0:T(8,128)} %left.1, f32[1,1,256,256]{3,2,1,0:T(8,128)} %right.1), custom_call_target="tpu_custom_call" | custom-call | flops 6442450944 | bytes 4194304 | tf_op jit(solution)/shard_map/two_site/pallas_call | solution.py:365
  83.4 2.3 %copy.7 = f32[1024,256]{1,0:T(8,128)} copy(f32[1024,256]{1,0:T(8,128)} %bitcast.1) | data formatting | bytes 2097152

commit v4 on v3

--- a/solution.py
+++ b/solution.py
@@ -143,10 +143,11 @@
     def spread(i, carry):
         p, i = div(i, 8), rem(i, 8)
         j = jnp.where(i == 7, 0, jnp.where(rem(i, 2) == 0, div(i, 2) + 1, 7 - div(i, 2)))
-        col = (2 * ypair + p) * Z + rem(z + j, Z)
+        s = rem(p + xodd, 2)
+        col = (2 * ypair + s) * Z + rem(z + j, Z)
         send(
             wave.at[quarter_rows, pl.ds(pl.multiple_of(col * SEC, SEC), SEC)],
-            wbuf.at[odd, p, quarter_rows], w_s.at[p, i], w_r.at[p, odd, quarter], w_to(j),
+            wbuf.at[odd, s, quarter_rows], w_s.at[p, i], w_r.at[s, odd, quarter], w_to(j),
             w_self & (i == 7))
         return carry
 
@@ -294,7 +295,8 @@
             (jnp.concatenate([h0, h1], 1), jnp.concatenate([l0, l1], 1)),
             (jnp.concatenate([rh0, rh1], 1), jnp.concatenate([rl0, rl1], 1)), (1, 1))
 
-    for s in range(2):
+    for p in range(2):
+        s = rem(p + xodd, 2)
         for e in (1 - odd, odd):
             inside = (row_at < ldims[x * Z + 2 * y + e]) & (col_at < rdims[(2 * c + s) * Z + z])
             for q in range(4):
@@ -307,7 +309,7 @@
             send(
                 acc.at[s, e], out.at[2 * yodd + e], o_s.at[s, e], o_r.at[2 * yodd + e],
                 device(2 * c + s, x, z, ypair), (x == y) & (c == ypair) & (xodd == s))
-            if s == 0 and e is not odd:
+            if p == 0 and e is not odd:
                 for n in (CHUNKS - 2, CHUNKS - 1):
                     arrive(n)
                 lax.fori_loop(issued(CHUNKS - 1), 16, spread, 0)

time: 85.8 us -> 85.3 us (level)
  no operation moved by 1% of the time
where the time goes in v4:
time: 85.3 us; the launch traced here: 85.1 us
  Pallas kernels  82.9 us (97%)
  local copies, waits for them, and re-layouts  2.26 us (3%)
    pallas_call x1, Pallas kernels, shards(): pl.pallas_call(kernel, out_shape=jax.ShapeDtypeStruct((4, SEC, SEC), F32)...  82.9 us
    unnamed x1, local copies, waits for them, and re-layouts  2.26 us

profile of v4, /device:TPU:35, one launch (start us, length us, event | category | flops | bytes accessed | tf_op | source)
XLA Modules:
  0.0 85.1 jit_solution(8837356005236072670)
XLA Ops:
  0.0 82.9 %two_site.1 = f32[4,256,256]{2,1,0:T(8,128)} custom-call(s32[32]{0:T(128)} %ldims.1, s32[32]{0:T(128)} %rdims.1, f32[256,8192]{1,0:T(8,128)} %wave.1, f32[1,1,256,256]{3,2,1,0:T(8,128)} %left.1, f32[1,1,256,256]{3,2,1,0:T(8,128)} %right.1), custom_call_target="tpu_custom_call" | custom-call | flops 6442450944 | bytes 4194304 | tf_op jit(solution)/shard_map/two_site/pallas_call | solution.py:367
  82.9 2.3 %copy.7 = f32[1024,256]{1,0:T(8,128)} copy(f32[1024,256]{1,0:T(8,128)} %bitcast.1) | data formatting | bytes 2097152
